TPU v7x, 32 devices: a whole 2x2x4 slice. The times are simulated.
32 devices in a mesh: region: 4 (over y, x), band: 8 (over z, core).
Axes of the slice: x: 2, y: 2, z: 4, core: 2. Of those that a mesh axis runs over, the one named last changes fastest.
Arguments:
- adjoint_in: float32 [128, 128, 512], P(None, 'band', 'region'), may hold values from -6 to 6
- courant_y: float32 [128, 128, 512], P(None, 'band', 'region'), may hold values from -0.45 to 0.45
- courant_x: float32 [128, 128, 512], P('band', None, 'region'), may hold values from -0.45 to 0.45
- diffusion_inverse: float32 [128, 128, 128], P('band')
- conv_weight: float32 [128, 512], P('band', 'region'), may hold values from 0.05 to 0.9
- cloud_base: int32 [128, 512], P('band', 'region'), may hold values from 0 to 63
- cloud_top: int32 [128, 512], P('band', 'region'), may hold values from 1 to 126, as said below
- sound_count: int32 [4, 64], P('region', 'band'), may hold values from 0 to 64, as said below
- xco2_adjoint: float32 [4, 64, 64], P('region', 'band'), may hold values from -6 to 6
- kernel: float32 [4, 64, 64, 128], P('region', 'band'), may hold values from 0.25 to 4
- sound_cols: int32 [4, 64, 64], P('region', 'band'), may hold values from 0 to 2047
Outputs:
- adjoint_out: float32 [128, 128, 512], P('band', None, 'region')
Inputs may be any that keep to these rules, and one draw needn't show every extreme that they name: `sound_count`: in every region one destination band receives 64 live slots from every source band. `sound_cols`: several slots may name the same column; the column is the latitude row within the band times 128 plus the longitude within the region. cloud_top > cloud_base in every column.
All inputs are finite; a program needn't handle non-finite values.
Results may differ from a plain program's by a relative error of at most 0.00014.
Values sent between devices are 32-bit elements; how exact they have to be, the bound alone decides.
A program may use at most 64 MiB of HBM per device.

v0:
```python
import jax
import jax.numpy as jnp
from jax import lax
from jax.sharding import PartitionSpec as P

YSTEPS = 2
XSTEPS = 4


def with_halo(cells, sides, width):
    for axis, dim in sides:
        count = lax.axis_size(axis)
        head = lax.slice_in_dim(cells, 0, width, axis=dim)
        tail = lax.slice_in_dim(cells, cells.shape[dim] - width, cells.shape[dim], axis=dim)
        cells = jnp.concatenate(
            [
                lax.ppermute(tail, axis, [(i, (i + 1) % count) for i in range(count)]),
                cells,
                lax.ppermute(head, axis, [((i + 1) % count, i) for i in range(count)]),
            ],
            axis=dim,
        )
    return cells


def take_next(field, dim):
    kept_part = lax.slice_in_dim(field, 1, field.shape[dim], axis=dim)
    zero_edge = jnp.zeros_like(lax.slice_in_dim(field, 0, 1, axis=dim))
    return jnp.concatenate([kept_part, zero_edge], axis=dim)


def take_prev(field, dim):
    kept_part = lax.slice_in_dim(field, 0, field.shape[dim] - 1, axis=dim)
    zero_edge = jnp.zeros_like(lax.slice_in_dim(field, 0, 1, axis=dim))
    return jnp.concatenate([zero_edge, kept_part], axis=dim)


def advect_sweep(tracer, courant, dim):
    outflow_up = jnp.maximum(courant, 0.0)
    lower_prev = take_prev(jnp.minimum(courant, 0.0), dim)
    return (
        (1.0 - outflow_up + lower_prev) * tracer
        + outflow_up * take_next(tracer, dim)
        - lower_prev * take_prev(tracer, dim)
    )


def vertical_mix(field, diffusion_inverse, conv_weight, cloud_base, cloud_top):
    levels = jnp.arange(field.shape[0], dtype=jnp.int32)[:, None, None]
    inside = ((levels >= cloud_base[None]) & (levels <= cloud_top[None])).astype(jnp.float32)
    cloud_depth = (cloud_top - cloud_base + 1).astype(jnp.float32)
    column_mean = jnp.sum(inside * field, axis=0) / cloud_depth
    convected = field + conv_weight[None] * inside * (column_mean[None] - field)
    return jnp.einsum("jlk,lji->kji", diffusion_inverse, convected, precision=lax.Precision.HIGHEST)


def lat_sweeps(pair_in):
    tracer, courant = pair_in
    row_count = tracer.shape[1]
    global_row = jnp.arange(row_count, dtype=jnp.int32)[None, :, None]
    courant_eff = jnp.where(global_row < row_count - 1, courant, 0.0)
    for substep in range(YSTEPS):
        tracer = advect_sweep(tracer, courant_eff, 1)
    return tracer


def per_device(
    adjoint_in,
    courant_y,
    courant_x,
    diffusion_inverse,
    conv_weight,
    cloud_base,
    cloud_top,
    sound_count,
    xco2_adjoint,
    kernel,
    sound_cols,
):
    levels, lat_rows, lon_cells = adjoint_in.shape
    slot_count = kernel.shape[2]
    slot_index = jnp.arange(slot_count, dtype=jnp.int32)
    live_slot = slot_index[None, None, :] < sound_count[:, :, None]
    partial_value = jnp.where(live_slot, xco2_adjoint, 0.0)[..., None] * kernel
    arrived = lax.all_to_all(partial_value, "band", split_axis=1, concat_axis=1, tiled=True)
    flat_cols = sound_cols.reshape(-1)
    update = arrived.reshape(-1, levels).T
    column = adjoint_in.reshape(levels, lat_rows * lon_cells)
    forced = column.at[:, flat_cols].add(update).reshape(adjoint_in.shape)
    mixed = vertical_mix(forced, diffusion_inverse, conv_weight, cloud_base, cloud_top)
    level_slab = lat_sweeps(
        (
            lax.all_to_all(mixed, "band", split_axis=0, concat_axis=1, tiled=True),
            lax.all_to_all(courant_y, "band", split_axis=0, concat_axis=1, tiled=True),
        )
    )
    extended = with_halo(jnp.stack([level_slab, courant_x]), (("region", 3),), XSTEPS)
    tracer = extended[0]
    for substep in range(XSTEPS):
        tracer = advect_sweep(tracer, extended[1], 2)
    result = tracer[:, :, XSTEPS : XSTEPS + lon_cells]
    return result


def solution(mesh):
    in_specs = (
        P(None, "band", "region"),
        P(None, "band", "region"),
        P("band", None, "region"),
        P("band", None, None),
        P("band", "region"),
        P("band", "region"),
        P("band", "region"),
        P("region", "band"),
        P("region", "band", None),
        P("region", "band", None, None),
        P("region", "band", None),
    )
    out_specs = P("band", None, "region")
    return jax.shard_map(
        per_device, mesh=mesh, in_specs=in_specs, out_specs=out_specs, check_vma=False
    )
```

profile of v0, /device:TPU:0, one launch (start us, length us, event | category | flops | bytes accessed | tf_op | source)
XLA Modules:
  0.0 111.7 jit_solution(12316257453905004826)
XLA Ops:
  0.0 0.0 copy-start
  0.0 0.0 copy-start.9
  0.0 0.0 copy-start.5
  0.0 0.9 select_bitcast_fusion
  0.9 1.1 bitcast_multiply_fusion
  2.0 15.9 %all_to_all.41 = f32[1,8,64,128]{3,2,0,1:T(8,128)S(1)} all-to-all(f32[1,8,64,128]{3,2,0,1:T(8,128)S(1)} %bitcast_multiply_fusion), channel_id=1, replica_groups=mesh['region'=4,'band'=8] {'band'}, dimensions={1} | all-to-all | bytes 524288 | tf_op jit(solution)/shard_map/all_to_all | solution.py:85
  17.9 4.2 %all-to-all-start = ((f32[128,16,128]{2,1,0:T(8,128)}), f32[128,16,128]{2,1,0:T(8,128)}, u32[]{:S(2)}, u32[]{:S(2)}) async-start(f32[128,16,128]{2,1,0:T(8,128)} %param.12), calls=%async_computation | async-start | bytes 2097152 | tf_op jit(solution)/shard_map/all_to_all | solution.py:94
  22.1 0.0 copy-done.9
  22.1 0.1 reshape.99
  22.2 0.0 copy-done.5
  22.2 0.4 copy.23
  22.7 0.0 copy-start.6
  22.7 0.0 copy-start.7
  22.7 0.0 copy-start.8
  22.7 3.7 %scatter_fusion = f32[128,2048]{0,1:T(8,128)S(1)} fusion(f32[128,2048]{0,1:T(8,128)S(1)} %bitcast.54, s32[512]{0:T(512)S(1)} %bitcast.62, f32[512,128]{1,0:T(8,128)S(1)} %bitcast.59), kind=kCustom, calls=%fused_computation | custom fusion | flops 65536 | bytes 788480 | tf_op jit(solution)/shard_map/scatter-add | solution.py:89
  26.4 0.0 copy-done.6
  26.4 0.0 copy-done.7
  26.4 1.0 select_reduce_fusion
  27.4 0.0 copy-done
  27.5 0.0 copy-done.8
  27.5 3.6 %convolution_bitcast_fusion = f32[128,16,128]{0,2,1:T(8,128)S(1)} fusion(f32[16,128,128]{2,1,0:T(8,128)S(1)} %copy-done, f32[128,16,128]{0,2,1:T(8,128)S(1)} %bitcast.55, f32[16,128]{1,0:T(8,128)S(1)} %bitcast_divide_fusion, f32[16,128]{1,0:T(8,128)S(1)} %copy-done.8, s32[16,128]{1,0:T(8,128)S(1)} %copy-done.6, s32[16,128]{1,0:T(8,128)S(1)} %copy-done.7), kind=kOutput, calls=%fused_computation.11 | convolution fusion | flops 404488192 | bytes 3178496 | tf_op jit(solution)/shard_map/jlk,lji->kji/dot_general | solution.py:54
  31.0 1.4 %copy.25 = f32[128,16,128]{2,1,0:T(8,128)} copy(f32[128,16,128]{0,2,1:T(8,128)S(1)} %convolution_bitcast_fusion) | data formatting | bytes 2097152 | tf_op jit(solution)/shard_map/jlk,lji->kji/transpose | solution.py:54
  32.4 16.3 %all-to-all-done = f32[128,16,128]{2,1,0:T(8,128)} async-done(((f32[128,16,128]{2,1,0:T(8,128)}), f32[128,16,128]{2,1,0:T(8,128)}, u32[]{:S(2)}, u32[]{:S(2)}) %all-to-all-start) | async-done | bytes 1048608 | tf_op jit(solution)/shard_map/all_to_all | solution.py:94
  48.7 4.2 %all-to-all-start.2 = ((f32[128,16,128]{2,1,0:T(8,128)}), f32[128,16,128]{2,1,0:T(8,128)}, u32[]{:S(2)}, u32[]{:S(2)}) async-start(f32[128,16,128]{2,1,0:T(8,128)} %copy.25), calls=%async_computation.2 | async-start | bytes 2097152 | tf_op jit(solution)/shard_map/all_to_all | solution.py:93
  53.0 1.3 %copy.22 = f32[8,16,16,128]{3,2,0,1:T(8,128)S(1)} copy(f32[8,16,16,128]{3,2,1,0:T(8,128)} %bitcast) | data formatting | bytes 2097152 | tf_op jit(solution)/shard_map/all_to_all | solution.py:94
  54.3 0.2 bitcast_select_fusion
  54.5 0.1 slice_minimum_fusion
  54.6 25.0 %all-to-all-done.2 = f32[128,16,128]{2,1,0:T(8,128)} async-done(((f32[128,16,128]{2,1,0:T(8,128)}), f32[128,16,128]{2,1,0:T(8,128)}, u32[]{:S(2)}, u32[]{:S(2)}) %all-to-all-start.2) | async-done | bytes 1048608 | tf_op jit(solution)/shard_map/all_to_all | solution.py:93
  79.6 1.3 %copy.26 = f32[16,8,16,128]{3,2,1,0:T(8,128)S(1)} copy(f32[16,8,16,128]{3,2,0,1:T(8,128)} %bitcast.15) | data formatting | bytes 2097152 | tf_op jit(solution)/shard_map/all_to_all | solution.py:93
  80.9 0.2 fusion.20
  81.1 0.7 multiply_subtract_fusion.3
  81.8 0.2 fusion.19
  82.0 0.0 copy-start.3
  82.0 0.7 subtract_bitcast_fusion
  82.7 0.0 copy-start.1
  82.7 0.5 copy-done.3
  83.3 2.1 %slice_maximum_fusion = (f32[2,16,128,4]{3,2,1,0:T(8,128)}, f32[2,16,128,4]{3,2,1,0:T(8,128)S(1)}) fusion(f32[1,16,128,128]{3,2,1,0:T(8,128)S(1)} %bitcast.57, f32[1,16,128,128]{3,2,1,0:T(8,128)S(1)} %subtract_bitcast_fusion), kind=kLoop, calls=%fused_computation.4 | loop fusion | flops 32768 | bytes 2228224 | tf_op jit(solution)/shard_map/stack | solution.py:97
  85.4 0.0 copy-done.1
  85.4 2.2 %copy.27 = f32[2,16,128,4]{2,1,3,0:T(8,128)S(1)} copy(f32[2,16,128,4]{3,2,1,0:T(8,128)} %get-tuple-element.18) | data formatting | bytes 131072 | tf_op jit(solution)/shard_map/slice | solution.py:14
  87.6 1.5 %collective-permute-start = (f32[2,16,128,4]{2,1,3,0:T(8,128)S(1)}, f32[2,16,128,4]{2,1,3,0:T(8,128)S(1)}, u32[]{:S(2)}, u32[]{:S(2)}) collective-permute-start(f32[2,16,128,4]{2,1,3,0:T(8,128)S(1)} %copy.27), channel_id=1, source_target_pairs={{0,8},{8,16},{16,24},{24,0},{1,9},{9,17},{17,25},{25,1},{2,10},{10... | collective-permute-start | bytes 196616 | tf_op jit(solution)/shard_map/ppermute | solution.py:17
  89.1 0.6 copy.28
  89.7 0.0 copy-start.2
  89.7 0.0 copy-start.4
  89.7 1.7 %collective-permute-start.1 = (f32[2,16,128,4]{2,1,3,0:T(8,128)S(1)}, f32[2,16,128,4]{2,1,3,0:T(8,128)S(1)}, u32[]{:S(2)}, u32[]{:S(2)}) collective-permute-start(f32[2,16,128,4]{2,1,3,0:T(8,128)S(1)} %copy.28), channel_id=1, source_target_pairs={{8,0},{16,8},{24,16},{0,24},{9,1},{17,9},{25,17},{1,25},{10,2},{18... | collective-permute-start | bytes 196616 | tf_op jit(solution)/shard_map/ppermute | solution.py:19
  91.4 1.4 %collective-permute-done = f32[2,16,128,4]{2,1,3,0:T(8,128)S(1)} collective-permute-done((f32[2,16,128,4]{2,1,3,0:T(8,128)S(1)}, f32[2,16,128,4]{2,1,3,0:T(8,128)S(1)}, u32[]{:S(2)}, u32[]{:S(2)}) %collective-permute-start) | collective-permute-done | bytes 65568 | tf_op jit(solution)/shard_map/ppermute | solution.py:17
  92.8 2.0 %copy.29 = f32[2,16,128,4]{3,2,1,0:T(8,128)} copy(f32[2,16,128,4]{2,1,3,0:T(8,128)S(1)} %collective-permute-done) | data formatting | bytes 131072 | tf_op jit(solution)/shard_map/ppermute | solution.py:17
  94.7 0.0 collective-permute-done.1
  94.7 2.0 %copy.30 = f32[2,16,128,4]{3,2,1,0:T(8,128)} copy(f32[2,16,128,4]{2,1,3,0:T(8,128)S(1)} %collective-permute-done.1) | data formatting | bytes 131072 | tf_op jit(solution)/shard_map/ppermute | solution.py:19
  96.7 0.0 copy-done.2
  96.7 0.0 copy-done.4
  96.7 3.9 %pad_maximum_fusion = f32[2,16,128,136]{3,2,1,0:T(8,128)S(1)} fusion(f32[2,16,128,4]{3,2,1,0:T(8,128)} %copy.30, f32[1,16,128,128]{3,2,1,0:T(8,128)S(1)} %bitcast.58, f32[1,16,128,128]{3,2,1,0:T(8,128)S(1)} %copy-done.2, f32[2,16,128,4]{3,2,1,0:T(8,128)} %copy.29), kind=kLoop, calls=%fused_computation.1 | loop fusion | flops 1671168 | bytes 4456448 | tf_op jit(solution)/shard_map/concatenate | solution.py:15
  100.6 0.8 maximum_bitcast_fusion
  101.4 0.8 fusion.18
  102.1 1.5 %subtract_add_fusion = (f32[16,128,136]{2,1,0:T(8,128)S(1)}, f32[16,128,136]{2,1,0:T(8,128)S(1)}) fusion(f32[16,128,135]{2,1,0:T(8,128)S(1)} %bitcast.50, f32[2,16,128,136]{3,2,1,0:T(8,128)S(1)} %pad_maximum_fusion, f32[16,128,135]{2,1,0:T(8,128)S(1)} %get-tuple-element.17, f32[16,128,135]{2,1,0:T(8,128)S(1)} %get-tuple-element.16), kind=kLoop, calls=%fused_computation.9 | loop fusion | flops 2228224 | bytes 7774208 | tf_op jit(solution)/shard_map/add | solution.py:42
  103.7 0.8 fusion.17
  104.4 1.5 %multiply_subtract_fusion.1 = f32[16,128,136]{2,1,0:T(8,128)S(1)} fusion(f32[16,128,135]{2,1,0:T(8,128)S(1)} %get-tuple-element.15, f32[16,128,135]{2,1,0:T(8,128)S(1)} %get-tuple-element.14, f32[16,128,136]{2,1,0:T(8,128)S(1)} %get-tuple-element.6, f32[16,128,135]{2,1,0:T(8,128)S(1)} %bitcast.51, f32[2,16,128,136]{3,2,1,0:T(8,128)S(1)} %pad_maximum_fusion), kind=kLoop, calls=%fused_computation.6 | loop fusion | flops 2228224 | bytes 6660096 | tf_op jit(solution)/shard_map/sub | solution.py:42
  105.9 0.7 fusion.16
  106.7 1.5 %multiply_subtract_fusion = f32[16,128,136]{2,1,0:T(8,128)S(1)} fusion(f32[16,128,135]{2,1,0:T(8,128)S(1)} %get-tuple-element.13, f32[16,128,135]{2,1,0:T(8,128)S(1)} %get-tuple-element.12, f32[16,128,136]{2,1,0:T(8,128)S(1)} %multiply_subtract_fusion.1, f32[16,128,135]{2,1,0:T(8,128)S(1)} %bitcast.52, f32[2,16,128,136]{3,2,1,0:T(8,128)S(1)} %pad_maximum_fusion), kind=kLoop, calls=%fused_computation.5 | loop fusion | flops 2228224 | bytes 6660096 | tf_op jit(solution)/shard_map/sub | solution.py:42
  108.2 0.7 fusion.15
  108.9 2.8 %fusion = f32[16,128,128]{2,1,0:T(8,128)} fusion(f32[16,128,135]{2,1,0:T(8,128)S(1)} %get-tuple-element.11, f32[16,128,135]{2,1,0:T(8,128)S(1)} %bitcast.53, f32[16,128,135]{2,1,0:T(8,128)S(1)} %get-tuple-element.10, f32[16,128,136]{2,1,0:T(8,128)S(1)} %get-tuple-element.7, f32[16,128,136]{2,1,0:T(8,128)S(1)} %multiply_subtract_fusion, ...), kind=kLoop, calls=%fused_computation.13 | loop fusion | flops 1310720 | bytes 7512064 | tf_op jit(solution)/shard_map/sub | solution.py:42
  (3 shorter events, 0.0 us)
Async XLA Ops:
  0.0 27.4 %copy-start = (f32[16,128,128]{2,1,0:T(8,128)S(1)}, f32[16,128,128]{2,1,0:T(8,128)}, u32[]{:S(2)}) copy-start(f32[16,128,128]{2,1,0:T(8,128)} %param.14) | copy-start | bytes 3145732
  0.0 22.1 %copy-start.9 = (s32[1,8,64]{2,1,0:T(8,128)S(1)}, s32[1,8,64]{2,1,0:T(8,128)}, u32[]{:S(2)}) copy-start(s32[1,8,64]{2,1,0:T(8,128)} %param.21) | copy-start | bytes 6148
  0.0 22.2 %copy-start.5 = (f32[128,16,128]{2,1,0:T(8,128)S(1)}, f32[128,16,128]{2,1,0:T(8,128)}, u32[]{:S(2)}) copy-start(f32[128,16,128]{2,1,0:T(8,128)} %param.11) | copy-start | bytes 3145732
  17.9 30.8 %all-to-all-start = ((f32[128,16,128]{2,1,0:T(8,128)}), f32[128,16,128]{2,1,0:T(8,128)}, u32[]{:S(2)}, u32[]{:S(2)}) async-start(f32[128,16,128]{2,1,0:T(8,128)} %param.12), calls=%async_computation | async-start | bytes 2097152 | tf_op jit(solution)/shard_map/all_to_all | solution.py:94
  22.7 3.7 %copy-start.6 = (s32[16,128]{1,0:T(8,128)S(1)}, s32[16,128]{1,0:T(8,128)}, u32[]{:S(2)}) copy-start(s32[16,128]{1,0:T(8,128)} %param.17) | copy-start | bytes 24580
  22.7 3.7 %copy-start.7 = (s32[16,128]{1,0:T(8,128)S(1)}, s32[16,128]{1,0:T(8,128)}, u32[]{:S(2)}) copy-start(s32[16,128]{1,0:T(8,128)} %param.16) | copy-start | bytes 24580
  22.7 4.8 %copy-start.8 = (f32[16,128]{1,0:T(8,128)S(1)}, f32[16,128]{1,0:T(8,128)}, u32[]{:S(2)}) copy-start(f32[16,128]{1,0:T(8,128)} %param.15) | copy-start | bytes 24580
  48.7 30.8 %all-to-all-start.2 = ((f32[128,16,128]{2,1,0:T(8,128)}), f32[128,16,128]{2,1,0:T(8,128)}, u32[]{:S(2)}, u32[]{:S(2)}) async-start(f32[128,16,128]{2,1,0:T(8,128)} %copy.25), calls=%async_computation.2 | async-start | bytes 2097152 | tf_op jit(solution)/shard_map/all_to_all | solution.py:93
  82.0 1.2 %copy-start.3 = (f32[16,128,128]{2,1,0:T(8,128)S(1)}, f32[16,128,128]{2,1,0:T(8,128)}, u32[]{:S(2)}) copy-start(f32[16,128,128]{2,1,0:T(8,128)} %param.13) | copy-start | bytes 3145732
  82.7 2.6 %copy-start.1 = (f32[1,16,128,128]{3,2,1,0:T(8,128)}, f32[1,16,128,128]{3,2,1,0:T(8,128)S(1)}, u32[]{:S(2)}) copy-start(f32[1,16,128,128]{3,2,1,0:T(8,128)S(1)} %subtract_bitcast_fusion) | copy-start | bytes 3145732
  87.6 5.2 %collective-permute-start = (f32[2,16,128,4]{2,1,3,0:T(8,128)S(1)}, f32[2,16,128,4]{2,1,3,0:T(8,128)S(1)}, u32[]{:S(2)}, u32[]{:S(2)}) collective-permute-start(f32[2,16,128,4]{2,1,3,0:T(8,128)S(1)} %copy.27), channel_id=1, source_target_pairs={{0,8},{8,16},{16,24},{24,0},{1,9},{9,17},{17,25},{25,1},{2,10},{10... | collective-permute-start | bytes 196616 | tf_op jit(solution)/shard_map/ppermute | solution.py:17
  89.7 7.0 %copy-start.2 = (f32[1,16,128,128]{3,2,1,0:T(8,128)S(1)}, f32[1,16,128,128]{3,2,1,0:T(8,128)}, u32[]{:S(2)}) copy-start(f32[1,16,128,128]{3,2,1,0:T(8,128)} %copy-done.1) | copy-start | bytes 3145732
  89.7 7.0 %copy-start.4 = (f32[16,128,128]{2,1,0:T(8,128)S(1)}, f32[16,128,128]{2,1,0:T(8,128)}, u32[]{:S(2)}) copy-start(f32[16,128,128]{2,1,0:T(8,128)} %param.13) | copy-start | bytes 3145732
  89.7 5.0 %collective-permute-start.1 = (f32[2,16,128,4]{2,1,3,0:T(8,128)S(1)}, f32[2,16,128,4]{2,1,3,0:T(8,128)S(1)}, u32[]{:S(2)}, u32[]{:S(2)}) collective-permute-start(f32[2,16,128,4]{2,1,3,0:T(8,128)S(1)} %copy.28), channel_id=1, source_target_pairs={{8,0},{16,8},{24,16},{0,24},{9,1},{17,9},{25,17},{1,25},{10,2},{18... | collective-permute-start | bytes 196616 | tf_op jit(solution)/shard_map/ppermute | solution.py:19
where the time goes:
time: 112 us
  waiting for transfers between devices  42.7 us (38%)
  other arithmetic  22.4 us (20%)
  blocking collectives  15.9 us (14%)
  local copies, waits for them, and re-layouts  15.2 us (14%)
  starting transfers between devices  11.7 us (10%)
  matrix products  3.56 us (3%)
    all_to_all x1, waiting for transfers between devices, per_device(): lax.all_to_all(mixed, 'band', split_axis=0, concat_axis=1, tiled=True)  25 us
    all_to_all x1, waiting for transfers between devices, per_device(): lax.all_to_all(courant_y, 'band', split_axis=0, concat_axis=1, tiled=True)  16.3 us
    all_to_all x1, blocking collectives, per_device(): lax.all_to_all(partial_value, 'band', split_axis=1, concat_axis=1, tiled=...  15.9 us
    sub x4, other arithmetic, advect_sweep(): (1.0 - outflow_up + lower_prev) * tracer  6.5 us
    all_to_all x1, starting transfers between devices, per_device(): lax.all_to_all(mixed, 'band', split_axis=0, concat_axis=1, tiled=True)  4.25 us
    all_to_all x1, starting transfers between devices, per_device(): lax.all_to_all(courant_y, 'band', split_axis=0, concat_axis=1, tiled=True)  4.25 us
    concatenate x1, other arithmetic, with_halo(): jnp.concatenate([lax.ppermute(tail, axis, [(i, (i + 1) % count) for i in...  3.91 us
    scatter-add x1, other arithmetic, per_device(): forced = column.at[:, flat_cols].add(update).reshape(adjoint_in.shape)  3.69 us
  transfers between devices with their start and end apart: 4, of which 3 were waited for; matrix products, arithmetic and copies ran while one was open for 13% of the time, Pallas kernels for 0%

commit v1 on v0

v1 whole, which is shorter than its diff:
```python
import functools

import jax
import jax.numpy as jnp
from jax import lax
from jax.experimental import pallas as pl
from jax.experimental.pallas import tpu as pltpu
from jax.sharding import PartitionSpec as P

XSTEPS = 4
PACK = 2 * XSTEPS
F32 = jnp.float32
BF16 = jnp.bfloat16


def split(x):
    hi = x.astype(BF16)
    return hi, (x - hi.astype(F32)).astype(BF16)


def step_kernel(
    nb, nr, lev, jb, ln, slots,
    adj, cy, cx, diff, conv_weight, base, top, count, xco2, kern, cols,
    out,
    ps, pr, onehot, ptb, dtb, mixed, mix_halo, cy_send, cy_halo,
    outgoing, arrived, cpack, cleft, cright, xpack, xleft, xright,
    s_send, s_recv, a_send, a_recv, h_send, h_recv, c_send, c_recv,
    l_send, l_recv, r_send, r_recv,
):
    lanes = 128
    n = ln * jb
    groups = lanes // PACK
    q = n // groups
    me = lax.axis_index("band")
    reg = lax.axis_index("region")
    right = lax.rem(reg + 1, nr)
    left = lax.rem(reg + nr - 1, nr)

    def partner(t):
        d, bit = 0, 1
        while bit < nb:
            d = d + bit * (((me // bit) % 2 + (t // bit) % 2) % 2)
            bit *= 2
        return d

    def to_band(src, dst, s_sem, r_sem, d):
        return pltpu.make_async_remote_copy(
            src_ref=src, dst_ref=dst, send_sem=s_sem, recv_sem=r_sem,
            device_id=(reg, d), device_id_type=pl.DeviceIdType.MESH)

    def to_region(src, dst, s_sem, r_sem, r):
        return pltpu.make_async_remote_copy(
            src_ref=src, dst_ref=dst, send_sem=s_sem, recv_sem=r_sem,
            device_id=(r, me), device_id_type=pl.DeviceIdType.MESH)

    barrier = pltpu.get_barrier_semaphore()
    for t in range(1, nb):
        pl.semaphore_signal(barrier, inc=1, device_id=(reg, partner(t)),
                            device_id_type=pl.DeviceIdType.MESH)
    for r in (left, right):
        pl.semaphore_signal(barrier, inc=1, device_id=(r, me),
                            device_id_type=pl.DeviceIdType.MESH)

    lane_row = lax.broadcasted_iota(jnp.int32, (1, slots), 1)
    eye = (lax.broadcasted_iota(jnp.int32, (slots, slots), 0)
           == lax.broadcasted_iota(jnp.int32, (slots, slots), 1))

    def as_column(row):
        return jnp.sum(jnp.where(eye, row, 0.0), axis=1, keepdims=True)

    for d in range(nb):
        w = jnp.where(lane_row < count[0, d], xco2[0, d:d + 1, :], 0.0)
        ps[d] = as_column(w) * kern[0, d]
    pr[me] = ps[me]

    pl.semaphore_wait(barrier, nb + 1)

    def sounding_copy(t):
        d = partner(t)
        return to_band(ps.at[d], pr.at[me], s_send.at[t], s_recv.at[t], d)

    for t in range(nb - 1, 0, -1):
        sounding_copy(t).start()

    cy_send[0] = cy[pl.ds(jb - 2, lev, stride=jb), :]
    cy_send[1] = cy[pl.ds(jb - 1, lev, stride=jb), :]
    cy_send[2] = cy[pl.ds(0, lev, stride=jb), :]

    def cy_up():
        return to_band(cy_send.at[pl.ds(0, 2)], cy_halo.at[pl.ds(0, 2)], h_send.at[0], h_recv.at[0], me + 1)

    def cy_down():
        return to_band(cy_send.at[pl.ds(2, 1)], cy_halo.at[pl.ds(2, 1)], h_send.at[1], h_recv.at[1], me - 1)

    def mix_up():
        return to_band(mixed.at[pl.ds(jb - 2, 2)], mix_halo.at[pl.ds(0, 2)], h_send.at[2], h_recv.at[2], me + 1)

    def mix_down():
        return to_band(mixed.at[pl.ds(0, 2)], mix_halo.at[pl.ds(2, 2)], h_send.at[3], h_recv.at[3], me - 1)

    has_next = me < nb - 1
    has_prev = me > 0

    @pl.when(has_next)
    def _():
        cy_up().start()

    @pl.when(has_prev)
    def _():
        cy_down().start()

    @pl.when(me == 0)
    def _():
        mix_halo[0:2] = jnp.zeros((2, lev, lanes), F32)
        cy_halo[0:2] = jnp.zeros((2, lev, lanes), F32)

    @pl.when(me == nb - 1)
    def _():
        mix_halo[2:4] = jnp.zeros((2, lev, lanes), F32)
        cy_halo[2:3] = jnp.zeros((1, lev, lanes), F32)

    lane = lax.broadcasted_iota(jnp.int32, (q, lanes), 1)
    lane_in = lane % PACK

    def pack(rows):
        total = jnp.zeros((q, lanes), F32)
        for g in range(groups):
            moved = pltpu.roll(rows(g), (XSTEPS + PACK * g) % lanes, 1)
            total = jnp.where(lane // PACK == g, moved, total)
        return total

    def cx_rows(s, g):
        k, jo = (g * q) // jb, (g * q) % jb
        return cx[k, pl.ds(pl.multiple_of(s * jb + jo, 8), q), :]

    def pack_courant(s, carry):
        cpack[s] = pack(lambda g: cx_rows(s, g))
        return carry

    lax.fori_loop(0, nb, pack_courant, 0)
    c_right = to_region(cpack, cleft, c_send.at[0], c_recv.at[0], right)
    c_left = to_region(cpack, cright, c_send.at[1], c_recv.at[1], left)
    c_right.start()
    c_left.start()

    cell = lax.broadcasted_iota(jnp.int32, (slots, lanes), 1).astype(F32)
    for s in range(nb):
        col = as_column(cols[0, s:s + 1, :].astype(F32))
        for j in range(jb):
            hit = jnp.where(col == cell + float(j * lanes), 1.0, 0.0)
            onehot[s * slots:(s + 1) * slots, j * lanes:(j + 1) * lanes] = hit.astype(BF16)

    def split_mix(j, carry):
        hi, lo = split(diff[j].T)
        dtb[j, :, 0:lev] = hi
        dtb[j, :, lev:2 * lev] = lo
        dtb[j, :, 2 * lev:3 * lev] = hi
        return carry

    lax.fori_loop(0, jb, split_mix, 0)

    for t in range(nb - 1, 0, -1):
        sounding_copy(t).wait_recv()
    for s in range(nb):
        hi, lo = split(pr[s].T)
        ptb[0:lev, s * slots:(s + 1) * slots] = hi
        ptb[lev:2 * lev, s * slots:(s + 1) * slots] = lo

    level = lax.broadcasted_iota(jnp.int32, (lev, lanes), 0)

    def mix_pair(jp):
        both = jnp.dot(ptb[...], onehot[:, pl.ds(pl.multiple_of(jp * 2 * lanes, 2 * lanes), 2 * lanes)],
                       preferred_element_type=F32)
        add = both[0:lev] + both[lev:2 * lev]
        for h in range(2):
            j = jp * 2 + h
            forced = adj[pl.ds(j, lev, stride=jb), :] + add[:, h * lanes:(h + 1) * lanes]
            lowest, highest = base[pl.ds(j, 1), :], top[pl.ds(j, 1), :]
            inside = (level >= lowest) & (level <= highest)
            depth = (highest - lowest + 1).astype(F32)
            mean = jnp.sum(jnp.where(inside, forced, 0.0), axis=0, keepdims=True) / depth
            conv = forced + jnp.where(inside, conv_weight[pl.ds(j, 1), :] * (mean - forced), 0.0)
            hi, lo = split(conv)
            mixed[j] = jnp.dot(dtb[j], jnp.concatenate([hi, hi, lo], axis=0), preferred_element_type=F32)

    mix_pair(0)

    @pl.when(has_prev)
    def _():
        mix_down().start()

    mix_pair(jb // 2 - 1)

    @pl.when(has_next)
    def _():
        mix_up().start()

    def mix_rest(jp, carry):
        mix_pair(jp)
        return carry

    lax.fori_loop(1, jb // 2 - 1, mix_rest, 0)

    @pl.when(has_next)
    def _():
        cy_down().wait_recv()
        mix_down().wait_recv()

    @pl.when(has_prev)
    def _():
        cy_up().wait_recv()
        mix_up().wait_recv()

    def sweep_y(d, store):
        ls = pl.ds(pl.multiple_of(d * ln, 8), ln)

        def field(r):
            if r < 2:
                return mix_halo[r, ls, :]
            if r < jb + 2:
                return mixed[r - 2, ls, :]
            return mix_halo[r - jb, ls, :]

        def courant(r):
            if r < 2:
                return cy_halo[r, ls, :]
            if r < jb + 2:
                c = cy[pl.ds(d * n + (r - 2), ln, stride=jb), :]
                return jnp.where(has_next, c, 0.0) if r == jb + 1 else c
            return cy_halo[2, ls, :]

        c_prev = jnp.minimum(courant(0), 0.0)
        a_prev, a_here = field(0), field(1)
        b_back = b_here = None
        coef = []
        for r in range(1, jb + 3):
            c_here = courant(r)
            a_next = field(r + 1)
            up = jnp.maximum(c_here, 0.0)
            mid = 1.0 - up + c_prev
            b_next = mid * a_here + up * a_next - c_prev * a_prev
            coef.append((mid, up, c_prev))
            if r >= 3:
                m2, u2, p2 = coef[-2]
                store(r - 3, m2 * b_here + u2 * b_next - p2 * b_back)
            b_back, b_here = b_here, b_next
            a_prev, a_here = a_here, a_next
            c_prev = jnp.minimum(c_here, 0.0)

    def block_copy(t):
        d = partner(t)
        return to_band(outgoing.at[pl.ds(pl.multiple_of(t * n, 8), n)],
                       arrived.at[pl.ds(pl.multiple_of(me * n, 8), n)],
                       a_send.at[t], a_recv.at[t], d)

    def send_block(i, carry):
        t = nb - 1 - i

        def store(j, value):
            outgoing[pl.ds(t * n + j, ln, stride=jb), :] = value

        sweep_y(partner(t), store)
        block_copy(t).start()
        return carry

    lax.fori_loop(0, nb - 1, send_block, 0)

    def store_own(j, value):
        arrived[pl.ds(me * n + j, ln, stride=jb), :] = value

    sweep_y(me, store_own)

    def halo_right(t):
        s = partner(t)
        return to_region(xpack.at[s], xleft.at[s], r_send.at[t], r_recv.at[t], right)

    def halo_left(t):
        s = partner(t)
        return to_region(xpack.at[s], xright.at[s], l_send.at[t], l_recv.at[t], left)

    def prepare(t):
        s = partner(t)
        xpack[s] = pack(lambda g: arrived[pl.ds(pl.multiple_of(s * n + g * q, 8), q), :])
        halo_right(t).start()
        halo_left(t).start()

    def finish(t):
        s = partner(t)
        halo_right(t).wait_recv()
        halo_left(t).wait_recv()
        low = lane_in < XSTEPS
        own, c_own = xpack[s], cpack[s]
        a = jnp.where(low, xleft[s], own)
        b = jnp.where(low, own, xright[s])
        ca = jnp.where(low, cleft[s], c_own)
        cb = jnp.where(low, c_own, cright[s])

        def coefs(c):
            up = jnp.maximum(c, 0.0)
            low_prev = pltpu.roll(jnp.minimum(c, 0.0), 1, 1)
            return 1.0 - up + low_prev, up, low_prev

        za, pa, ma = coefs(ca)
        zb, pb, mb = coefs(cb)
        edges = []
        for step in range(XSTEPS):
            a_prev, b_next = pltpu.roll(a, 1, 1), pltpu.roll(b, lanes - 1, 1)
            edges.append(jnp.where(lane_in == XSTEPS, a_prev, b_next))
            if step < XSTEPS - 1:
                a = za * a + pa * pltpu.roll(a, lanes - 1, 1) - ma * a_prev
                b = zb * b + pb * b_next - mb * pltpu.roll(b, 1, 1)
        first, last = lane == 0, lane == lanes - 1
        for g in range(groups):
            back = (lanes - XSTEPS - PACK * g) % lanes
            x = arrived[pl.ds(pl.multiple_of(s * n + g * q, 8), q), :]
            c = cx_rows(s, g)
            up = jnp.maximum(c, 0.0)
            low_prev = jnp.where(first, pltpu.roll(ma, back, 1), pltpu.roll(jnp.minimum(c, 0.0), 1, 1))
            mid = 1.0 - up + low_prev
            for step in range(XSTEPS):
                edge = pltpu.roll(edges[step], back, 1)
                nxt = jnp.where(last, edge, pltpu.roll(x, lanes - 1, 1))
                prv = jnp.where(first, edge, pltpu.roll(x, 1, 1))
                x = mid * x + up * nxt - low_prev * prv
            k, jo = (g * q) // jb, (g * q) % jb
            out[k, pl.ds(pl.multiple_of(s * jb + jo, 8), q), :] = x

    prepare(0)
    c_right.wait_recv()
    c_left.wait_recv()

    def drain(i, carry):
        t = nb - i
        block_copy(t).wait_recv()
        prepare(t)
        finish((t + 1) % nb)
        return carry

    lax.fori_loop(1, nb, drain, 0)
    finish(1)

    c_right.wait_send()
    c_left.wait_send()

    @pl.when(has_next)
    def _():
        cy_up().wait_send()
        mix_up().wait_send()

    @pl.when(has_prev)
    def _():
        cy_down().wait_send()
        mix_down().wait_send()

    def finish_sends(t, carry):
        halo_right(t).wait_send()
        halo_left(t).wait_send()
        return carry

    lax.fori_loop(0, nb, finish_sends, 0)

    def finish_blocks(t, carry):
        sounding_copy(t).wait_send()
        block_copy(t).wait_send()
        return carry

    lax.fori_loop(1, nb, finish_blocks, 0)


def per_device(nb, nr, adj, cy, cx, diff, conv_weight, base, top, count, xco2, kern, cols):
    lev, jb, lanes = adj.shape
    ln, lat, _ = cx.shape
    slots = kern.shape[2]
    n = ln * jb
    q = n * PACK // lanes
    vmem = pl.BlockSpec(memory_space=pltpu.VMEM)
    smem = pl.BlockSpec(memory_space=pltpu.SMEM)
    dma = pltpu.SemaphoreType.DMA
    rows = (nb, q, lanes)
    return pl.pallas_call(
        functools.partial(step_kernel, nb, nr, lev, jb, ln, slots),
        out_shape=jax.ShapeDtypeStruct((ln, lat, lanes), F32),
        in_specs=[vmem] * 7 + [smem] + [vmem] * 3,
        out_specs=vmem,
        scratch_shapes=[
            pltpu.VMEM((nb, slots, lev), F32),
            pltpu.VMEM((nb, slots, lev), F32),
            pltpu.VMEM((nb * slots, jb * lanes), BF16),
            pltpu.VMEM((2 * lev, nb * slots), BF16),
            pltpu.VMEM((jb, lev, 3 * lev), BF16),
            pltpu.VMEM((jb, lev, lanes), F32),
            pltpu.VMEM((4, lev, lanes), F32),
            pltpu.VMEM((3, lev, lanes), F32),
            pltpu.VMEM((3, lev, lanes), F32),
            pltpu.VMEM((nb * n, lanes), F32),
            pltpu.VMEM((nb * n, lanes), F32),
            pltpu.VMEM(rows, F32), pltpu.VMEM(rows, F32), pltpu.VMEM(rows, F32),
            pltpu.VMEM(rows, F32), pltpu.VMEM(rows, F32), pltpu.VMEM(rows, F32),
            dma((nb,)), dma((nb,)), dma((nb,)), dma((nb,)),
            dma((4,)), dma((4,)), dma((2,)), dma((2,)),
            dma((nb,)), dma((nb,)), dma((nb,)), dma((nb,)),
        ],
        compiler_params=pltpu.CompilerParams(
            collective_id=0, has_side_effects=True, vmem_limit_bytes=48 * 1024 * 1024),
    )(adj.reshape(lev * jb, lanes), cy.reshape(lev * jb, lanes), cx, diff,
      conv_weight, base, top, count, xco2, kern, cols)


def solution(mesh):
    in_specs = (
        P(None, "band", "region"),
        P(None, "band", "region"),
        P("band", None, "region"),
        P("band", None, None),
        P("band", "region"),
        P("band", "region"),
        P("band", "region"),
        P("region", "band"),
        P("region", "band", None),
        P("region", "band", None, None),
        P("region", "band", None),
    )
    run = functools.partial(per_device, mesh.shape["band"], mesh.shape["region"])
    return jax.shard_map(
        run, mesh=mesh, in_specs=in_specs, out_specs=P("band", None, "region"), check_vma=False
    )
```

time: 112 us -> 67.2 us (0.60)
  Pallas kernels: 0 us -> 55.8 us
  waiting for transfers between devices: 42.7 us -> 0 us
  other arithmetic: 22.4 us -> 0 us
  blocking collectives: 15.9 us -> 0 us
  starting transfers between devices: 11.7 us -> 0 us
  local copies, waits for them, and re-layouts: 15.2 us -> 10.9 us
  matrix products: 3.56 us -> 0 us
    pallas_call x0 -> x1, Pallas kernels: none -> 55.8 us  [per_device(): pl.pallas_call(functools.partial(step_kernel, nb, nr, lev, jb, ln, slots)...]
    all_to_all x2 -> x0, waiting for transfers between devices: 41.3 us -> none  [the longest x1 25 us: per_device(): lax.all_to_all(mixed, 'band', split_axis=0, concat_axis=1, tiled=True)]
    all_to_all x1 -> x0, blocking collectives: 15.9 us -> none  [per_device(): lax.all_to_all(partial_value, 'band', split_axis=1, concat_axis=1, tiled=...]
    unnamed x21 -> x23, local copies, waits for them, and re-layouts: 0.99 us -> 10.9 us
    all_to_all x2 -> x0, starting transfers between devices: 8.5 us -> none  [the longest x1 4.25 us: per_device(): lax.all_to_all(mixed, 'band', split_axis=0, concat_axis=1, tiled=True)]
    sub x4 -> x0, other arithmetic: 6.5 us -> none  [advect_sweep(): (1.0 - outflow_up + lower_prev) * tracer]
    slice x8 -> x0, local copies, waits for them, and re-layouts: 6.2 us -> none  [the longest x6 3.38 us: take_next(): kept_part = lax.slice_in_dim(field, 1, field.shape[dim], axis=dim)]
    ppermute x2 -> x0, local copies, waits for them, and re-layouts: 3.94 us -> none  [the longest x1 1.98 us: with_halo(): lax.ppermute(head, axis, [((i + 1) % count, i) for i in range(count)])]
  transfers between devices with their start and end apart: 4 -> 0, of which waited for: 3 -> 0; matrix products, arithmetic and copies ran while one was open for 13% -> 0% of each run, Pallas kernels for 0% -> 0%
where the time goes in v1:
time: 67.2 us; the launch traced here: 66.7 us
  Pallas kernels  55.8 us (83%)
  local copies, waits for them, and re-layouts  10.9 us (16%)
    pallas_call x1, Pallas kernels, per_device(): pl.pallas_call(functools.partial(step_kernel, nb, nr, lev, jb, ln, slots)...  55.8 us
    unnamed x23, local copies, waits for them, and re-layouts  10.9 us

profile of v1, /device:TPU:0, one launch (start us, length us, event | category | flops | bytes accessed | tf_op | source)
XLA Modules:
  0.0 66.7 jit_solution(4543915015074270083)
XLA Ops:
  0.0 0.0 copy-start.10
  0.0 0.7 copy-done.10
  0.7 0.0 copy-start
  0.7 1.2 %copy-done = f32[128,16,128]{2,1,0:T(8,128)S(1)} copy-done((f32[128,16,128]{2,1,0:T(8,128)S(1)}, f32[128,16,128]{2,1,0:T(8,128)}, u32[]{:S(2)}) %copy-start) | copy-done | bytes 1048600
  1.9 0.0 copy-start.1
  1.9 1.2 %copy-done.1 = f32[128,16,128]{2,1,0:T(8,128)S(1)} copy-done((f32[128,16,128]{2,1,0:T(8,128)S(1)}, f32[128,16,128]{2,1,0:T(8,128)}, u32[]{:S(2)}) %copy-start.1) | copy-done | bytes 1048600
  3.1 0.0 copy-start.2
  3.1 1.2 %copy-done.2 = f32[16,128,128]{2,1,0:T(8,128)S(1)} copy-done((f32[16,128,128]{2,1,0:T(8,128)S(1)}, f32[16,128,128]{2,1,0:T(8,128)}, u32[]{:S(2)}) %copy-start.2) | copy-done | bytes 1048600
  4.3 0.0 copy-start.3
  4.3 1.2 %copy-done.3 = f32[16,128,128]{2,1,0:T(8,128)S(1)} copy-done((f32[16,128,128]{2,1,0:T(8,128)S(1)}, f32[16,128,128]{2,1,0:T(8,128)}, u32[]{:S(2)}) %copy-start.3) | copy-done | bytes 1048600
  5.6 0.0 copy-start.4
  5.6 0.9 %copy-done.4 = f32[1,8,64,128]{3,2,1,0:T(8,128)S(1)} copy-done((f32[1,8,64,128]{3,2,1,0:T(8,128)S(1)}, f32[1,8,64,128]{3,2,1,0:T(8,128)}, u32[]{:S(2)}) %copy-start.4) | copy-done | bytes 262168
  6.5 0.0 copy-start.5
  6.5 0.7 %copy-done.5 = f32[16,128]{1,0:T(8,128)S(1)} copy-done((f32[16,128]{1,0:T(8,128)S(1)}, f32[16,128]{1,0:T(8,128)}, u32[]{:S(2)}) %copy-start.5) | copy-done | bytes 8216
  7.2 0.0 copy-start.6
  7.2 0.7 %copy-done.6 = s32[16,128]{1,0:T(8,128)S(1)} copy-done((s32[16,128]{1,0:T(8,128)S(1)}, s32[16,128]{1,0:T(8,128)}, u32[]{:S(2)}) %copy-start.6) | copy-done | bytes 8216
  7.9 0.0 copy-start.7
  7.9 0.7 %copy-done.7 = s32[16,128]{1,0:T(8,128)S(1)} copy-done((s32[16,128]{1,0:T(8,128)S(1)}, s32[16,128]{1,0:T(8,128)}, u32[]{:S(2)}) %copy-start.7) | copy-done | bytes 8216
  8.6 0.0 copy-start.8
  8.6 0.7 %copy-done.8 = f32[1,8,64]{2,1,0:T(8,128)S(1)} copy-done((f32[1,8,64]{2,1,0:T(8,128)S(1)}, f32[1,8,64]{2,1,0:T(8,128)}, u32[]{:S(2)}) %copy-start.8) | copy-done | bytes 2072
  9.3 0.0 copy-start.9
  9.3 0.7 %copy-done.9 = s32[1,8,64]{2,1,0:T(8,128)S(1)} copy-done((s32[1,8,64]{2,1,0:T(8,128)S(1)}, s32[1,8,64]{2,1,0:T(8,128)}, u32[]{:S(2)}) %copy-start.9) | copy-done | bytes 2072
  10.0 55.8 %shard_map.109 = f32[16,128,128]{2,1,0:T(8,128)S(1)} custom-call(f32[2048,128]{1,0:T(8,128)S(1)} %bitcast.2, f32[2048,128]{1,0:T(8,128)S(1)} %bitcast.3, f32[16,128,128]{2,1,0:T(8,128)S(1)} %copy-done.2, f32[16,128,128]{2,1,0:T(8,128)S(1)} %copy-done.3, f32[16,128]{1,0:T(8,128)S(1)} %copy-done.5, s32[16,128]{1,0:T(8,128)S(1)} %copy-done.6, ...), custom_call_target="tpu_custom_call" | custom-call | tf_op jit(solution)/shard_map/pallas_call | solution.py:380
  65.8 1.0 %copy.13 = f32[16,128,128]{2,1,0:T(8,128)} copy(f32[16,128,128]{2,1,0:T(8,128)S(1)} %shard_map.109) | data formatting | bytes 2097152
Async XLA Ops:
  0.0 0.7 copy-start.10
  0.7 1.2 %copy-start = (f32[128,16,128]{2,1,0:T(8,128)S(1)}, f32[128,16,128]{2,1,0:T(8,128)}, u32[]{:S(2)}) copy-start(f32[128,16,128]{2,1,0:T(8,128)} %param.11) | copy-start | bytes 3145732
  1.9 1.2 %copy-start.1 = (f32[128,16,128]{2,1,0:T(8,128)S(1)}, f32[128,16,128]{2,1,0:T(8,128)}, u32[]{:S(2)}) copy-start(f32[128,16,128]{2,1,0:T(8,128)} %param.12) | copy-start | bytes 3145732
  3.1 1.2 %copy-start.2 = (f32[16,128,128]{2,1,0:T(8,128)S(1)}, f32[16,128,128]{2,1,0:T(8,128)}, u32[]{:S(2)}) copy-start(f32[16,128,128]{2,1,0:T(8,128)} %cx.1) | copy-start | bytes 3145732
  4.3 1.2 %copy-start.3 = (f32[16,128,128]{2,1,0:T(8,128)S(1)}, f32[16,128,128]{2,1,0:T(8,128)}, u32[]{:S(2)}) copy-start(f32[16,128,128]{2,1,0:T(8,128)} %diff.1) | copy-start | bytes 3145732
  5.6 0.9 %copy-start.4 = (f32[1,8,64,128]{3,2,1,0:T(8,128)S(1)}, f32[1,8,64,128]{3,2,1,0:T(8,128)}, u32[]{:S(2)}) copy-start(f32[1,8,64,128]{3,2,1,0:T(8,128)} %kern.1) | copy-start | bytes 786436
  6.5 0.7 %copy-start.5 = (f32[16,128]{1,0:T(8,128)S(1)}, f32[16,128]{1,0:T(8,128)}, u32[]{:S(2)}) copy-start(f32[16,128]{1,0:T(8,128)} %conv_weight.1) | copy-start | bytes 24580
  7.2 0.7 %copy-start.6 = (s32[16,128]{1,0:T(8,128)S(1)}, s32[16,128]{1,0:T(8,128)}, u32[]{:S(2)}) copy-start(s32[16,128]{1,0:T(8,128)} %base.1) | copy-start | bytes 24580
  7.9 0.7 %copy-start.7 = (s32[16,128]{1,0:T(8,128)S(1)}, s32[16,128]{1,0:T(8,128)}, u32[]{:S(2)}) copy-start(s32[16,128]{1,0:T(8,128)} %top.1) | copy-start | bytes 24580
  8.6 0.7 %copy-start.8 = (f32[1,8,64]{2,1,0:T(8,128)S(1)}, f32[1,8,64]{2,1,0:T(8,128)}, u32[]{:S(2)}) copy-start(f32[1,8,64]{2,1,0:T(8,128)} %xco2.1) | copy-start | bytes 6148
  9.3 0.7 %copy-start.9 = (s32[1,8,64]{2,1,0:T(8,128)S(1)}, s32[1,8,64]{2,1,0:T(8,128)}, u32[]{:S(2)}) copy-start(s32[1,8,64]{2,1,0:T(8,128)} %cols.1) | copy-start | bytes 6148

commit v2 on v1

--- a/solution.py
+++ b/solution.py
@@ -20,8 +20,9 @@
 
 def step_kernel(
     nb, nr, lev, jb, ln, slots,
-    adj, cy, cx, diff, conv_weight, base, top, count, xco2, kern, cols,
+    adj_hbm, cy_hbm, cx_hbm, diff_hbm, conv_hbm, base_hbm, top_hbm, count_hbm, xco2_hbm, kern_hbm, cols_hbm,
     out,
+    adj, cy, cx, diff, conv_weight, base, top, count, xco2, kern, cols, in_sem,
     ps, pr, onehot, ptb, dtb, mixed, mix_halo, cy_send, cy_halo,
     outgoing, arrived, cpack, cleft, cright, xpack, xleft, xright,
     s_send, s_recv, a_send, a_recv, h_send, h_recv, c_send, c_recv,
@@ -29,6 +30,14 @@
 ):
     lanes = 128
     n = ln * jb
+    loads = {}
+    for slot, (name, src, dst) in enumerate((
+        ("kern", kern_hbm, kern), ("xco2", xco2_hbm, xco2), ("count", count_hbm, count),
+        ("cy", cy_hbm, cy), ("cx", cx_hbm, cx), ("cols", cols_hbm, cols), ("diff", diff_hbm, diff),
+        ("adj", adj_hbm, adj), ("conv", conv_hbm, conv_weight), ("base", base_hbm, base), ("top", top_hbm, top),
+    )):
+        loads[name] = pltpu.make_async_copy(src, dst, in_sem.at[slot])
+        loads[name].start()
     groups = lanes // PACK
     q = n // groups
     me = lax.axis_index("band")
@@ -68,8 +77,11 @@
     def as_column(row):
         return jnp.sum(jnp.where(eye, row, 0.0), axis=1, keepdims=True)
 
+    for name in ("kern", "xco2", "count"):
+        loads[name].wait()
+
     for d in range(nb):
-        w = jnp.where(lane_row < count[0, d], xco2[0, d:d + 1, :], 0.0)
+        w = jnp.where(lane_row < count[0:1, d:d + 1], xco2[0, d:d + 1, :], 0.0)
         ps[d] = as_column(w) * kern[0, d]
     pr[me] = ps[me]
 
@@ -81,6 +93,8 @@
 
     for t in range(nb - 1, 0, -1):
         sounding_copy(t).start()
+
+    loads["cy"].wait()
 
     cy_send[0] = cy[pl.ds(jb - 2, lev, stride=jb), :]
     cy_send[1] = cy[pl.ds(jb - 1, lev, stride=jb), :]
@@ -137,11 +151,15 @@
         cpack[s] = pack(lambda g: cx_rows(s, g))
         return carry
 
+    loads["cx"].wait()
     lax.fori_loop(0, nb, pack_courant, 0)
     c_right = to_region(cpack, cleft, c_send.at[0], c_recv.at[0], right)
     c_left = to_region(cpack, cright, c_send.at[1], c_recv.at[1], left)
     c_right.start()
     c_left.start()
+
+    loads["cols"].wait()
+    loads["diff"].wait()
 
     cell = lax.broadcasted_iota(jnp.int32, (slots, lanes), 1).astype(F32)
     for s in range(nb):
@@ -165,6 +183,9 @@
         hi, lo = split(pr[s].T)
         ptb[0:lev, s * slots:(s + 1) * slots] = hi
         ptb[lev:2 * lev, s * slots:(s + 1) * slots] = lo
+
+    for name in ("adj", "conv", "base", "top"):
+        loads[name].wait()
 
     level = lax.broadcasted_iota(jnp.int32, (lev, lanes), 0)
 
@@ -330,14 +351,13 @@
     c_left.wait_recv()
 
     def drain(i, carry):
-        t = nb - i
-        block_copy(t).wait_recv()
-        prepare(t)
-        finish((t + 1) % nb)
+        block_copy(i).wait_recv()
+        prepare(i)
+        finish(i - 1)
         return carry
 
     lax.fori_loop(1, nb, drain, 0)
-    finish(1)
+    finish(nb - 1)
 
     c_right.wait_send()
     c_left.wait_send()
@@ -374,15 +394,18 @@
     n = ln * jb
     q = n * PACK // lanes
     vmem = pl.BlockSpec(memory_space=pltpu.VMEM)
-    smem = pl.BlockSpec(memory_space=pltpu.SMEM)
+    hbm = pl.BlockSpec(memory_space=pltpu.HBM)
+    operands = (adj.reshape(lev * jb, lanes), cy.reshape(lev * jb, lanes), cx, diff,
+                conv_weight, base, top, count, xco2, kern, cols)
     dma = pltpu.SemaphoreType.DMA
     rows = (nb, q, lanes)
     return pl.pallas_call(
         functools.partial(step_kernel, nb, nr, lev, jb, ln, slots),
         out_shape=jax.ShapeDtypeStruct((ln, lat, lanes), F32),
-        in_specs=[vmem] * 7 + [smem] + [vmem] * 3,
+        in_specs=[hbm] * len(operands),
         out_specs=vmem,
-        scratch_shapes=[
+        scratch_shapes=[pltpu.VMEM(x.shape, x.dtype) for x in operands] + [
+            dma((len(operands),)),
             pltpu.VMEM((nb, slots, lev), F32),
             pltpu.VMEM((nb, slots, lev), F32),
             pltpu.VMEM((nb * slots, jb * lanes), BF16),
@@ -401,9 +424,8 @@
             dma((nb,)), dma((nb,)), dma((nb,)), dma((nb,)),
         ],
         compiler_params=pltpu.CompilerParams(
-            collective_id=0, has_side_effects=True, vmem_limit_bytes=48 * 1024 * 1024),
-    )(adj.reshape(lev * jb, lanes), cy.reshape(lev * jb, lanes), cx, diff,
-      conv_weight, base, top, count, xco2, kern, cols)
+            collective_id=0, has_side_effects=True, vmem_limit_bytes=63 * 1024 * 1024),
+    )(*operands)
 
 
 def solution(mesh):

time: 67.2 us -> 56.3 us (0.84)
  local copies, waits for them, and re-layouts: 10.9 us -> 2.3 us
  Pallas kernels: 55.8 us -> 53.9 us
    unnamed x23 -> x1, local copies, waits for them, and re-layouts: 10.9 us -> 2.3 us
    pallas_call x1, Pallas kernels: 55.8 us -> 53.9 us  [per_device(): pl.pallas_call(functools.partial(step_kernel, nb, nr, lev, jb, ln, slots)...]
where the time goes in v2:
time: 56.3 us; the launch traced here: 56.2 us
  Pallas kernels  53.9 us (96%)
  local copies, waits for them, and re-layouts  2.3 us (4%)
    pallas_call x1, Pallas kernels, per_device(): pl.pallas_call(functools.partial(step_kernel, nb, nr, lev, jb, ln, slots)...  53.9 us
    unnamed x1, local copies, waits for them, and re-layouts  2.3 us

profile of v2, /device:TPU:0, one launch (start us, length us, event | category | flops | bytes accessed | tf_op | source)
XLA Modules:
  0.0 56.2 jit_solution(702194760838923684)
XLA Ops:
  0.0 53.9 %shard_map.109 = f32[16,128,128]{2,1,0:T(8,128)} custom-call(f32[2048,128]{1,0:T(8,128)} %bitcast.2, f32[2048,128]{1,0:T(8,128)} %bitcast.3, f32[16,128,128]{2,1,0:T(8,128)} %cx_hbm.1, f32[16,128,128]{2,1,0:T(8,128)} %diff_hbm.1, f32[16,128]{1,0:T(8,128)} %conv_hbm.1, s32[16,128]{1,0:T(8,128)} %base_hbm.1, s32[16,128]{1,0:T(8,128)} %top_hbm.1, ...), custom_call_target="tpu_custom_call" | custom-call | tf_op jit(solution)/shard_map/pallas_call | solution.py:402
  53.9 2.3 %copy.13 = f32[16,128,128]{2,1,0:T(8,128)} copy(f32[16,128,128]{2,1,0:T(8,128)} %shard_map.109) | data formatting | bytes 2097152

commit v3 on v2

--- a/solution.py
+++ b/solution.py
@@ -9,6 +9,7 @@
 
 XSTEPS = 4
 PACK = 2 * XSTEPS
+LAG = 2
 F32 = jnp.float32
 BF16 = jnp.bfloat16
 
@@ -275,7 +276,7 @@
                        a_send.at[t], a_recv.at[t], d)
 
     def send_block(i, carry):
-        t = nb - 1 - i
+        t = (i // 2 + 1) + ((i + 1) % 2) * (nb // 2 - 1)
 
         def store(j, value):
             outgoing[pl.ds(t * n + j, ln, stride=jb), :] = value
@@ -347,17 +348,25 @@
             out[k, pl.ds(pl.multiple_of(s * jb + jo, 8), q), :] = x
 
     prepare(0)
+    for t in range(1, LAG):
+        block_copy(t).wait_recv()
+        prepare(t)
     c_right.wait_recv()
     c_left.wait_recv()
 
     def drain(i, carry):
         block_copy(i).wait_recv()
         prepare(i)
-        finish(i - 1)
-        return carry
-
-    lax.fori_loop(1, nb, drain, 0)
-    finish(nb - 1)
+        finish(i - LAG)
+        return carry
+
+    lax.fori_loop(LAG, nb, drain, 0)
+
+    def finish_rest(t, carry):
+        finish(t)
+        return carry
+
+    lax.fori_loop(nb - LAG, nb, finish_rest, 0)
 
     c_right.wait_send()
     c_left.wait_send()

time: 56.3 us -> 49.9 us (0.89)
  Pallas kernels: 53.9 us -> 47.4 us
    pallas_call x1, Pallas kernels: 53.9 us -> 47.4 us  [per_device(): pl.pallas_call(functools.partial(step_kernel, nb, nr, lev, jb, ln, slots)...]
where the time goes in v3:
time: 49.9 us; the launch traced here: 49.7 us
  Pallas kernels  47.4 us (95%)
  local copies, waits for them, and re-layouts  2.3 us (5%)
    pallas_call x1, Pallas kernels, per_device(): pl.pallas_call(functools.partial(step_kernel, nb, nr, lev, jb, ln, slots)...  47.4 us
    unnamed x1, local copies, waits for them, and re-layouts  2.3 us

profile of v3, /device:TPU:0, one launch (start us, length us, event | category | flops | bytes accessed | tf_op | source)
XLA Modules:
  0.0 49.7 jit_solution(16635061638571326795)
XLA Ops:
  0.0 47.4 %shard_map.109 = f32[16,128,128]{2,1,0:T(8,128)} custom-call(f32[2048,128]{1,0:T(8,128)} %bitcast.2, f32[2048,128]{1,0:T(8,128)} %bitcast.3, f32[16,128,128]{2,1,0:T(8,128)} %cx_hbm.1, f32[16,128,128]{2,1,0:T(8,128)} %diff_hbm.1, f32[16,128]{1,0:T(8,128)} %conv_hbm.1, s32[16,128]{1,0:T(8,128)} %base_hbm.1, s32[16,128]{1,0:T(8,128)} %top_hbm.1, ...), custom_call_target="tpu_custom_call" | custom-call | tf_op jit(solution)/shard_map/pallas_call | solution.py:411
  47.4 2.3 %copy.13 = f32[16,128,128]{2,1,0:T(8,128)} copy(f32[16,128,128]{2,1,0:T(8,128)} %shard_map.109) | data formatting | bytes 2097152
